TPU v7x, 32 devices: a whole 2x2x4 slice. The times are simulated.
32 devices in a mesh: parts: 2 (over y), branch: 4 (over z), sub: 4 (over x, core).
Axes of the slice: x: 2, y: 2, z: 4, core: 2. Of those that a mesh axis runs over, the one named last changes fastest.
Arguments:
- charges: bfloat16 [2048, 64, 128], P(('parts', 'branch', 'sub')), parts along dimension 0, may hold values from -6 to 6
- leaf_basis: bfloat16 [2048, 64, 64], P(('parts', 'branch', 'sub')), parts along dimension 0, may hold values from -0.75 to 0.75
- leaf_transfer: bfloat16 [2048, 64, 64], P(('parts', 'branch', 'sub')), parts along dimension 0, may hold values from -0.375 to 0.375
- parent_transfer: bfloat16 [512, 64, 64], P(('parts', 'branch', 'sub')), parts along dimension 0, may hold values from -0.375 to 0.375
- near_source: int32 [2048, 8], P(('parts', 'branch', 'sub')), parts along dimension 0, may hold values from 0 to 1023, as said below
- near_block: bfloat16 [2048, 8, 64, 64], P(('parts', 'branch', 'sub')), parts along dimension 0, may hold values from -0.25 to 0.25
- local_source: int32 [2048, 4], P(('parts', 'branch', 'sub')), parts along dimension 0, may hold values from 0 to 1023, as said below
- local_count: int32 [2048], P(('parts', 'branch', 'sub')), parts along dimension 0, may hold values from 1 to 4, as said below
- local_coupling: bfloat16 [2048, 4, 64, 64], P(('parts', 'branch', 'sub')), parts along dimension 0, may hold values from -0.375 to 0.375
- remote_target: int32 [32, 32], P(('parts', 'branch', 'sub')), parts along dimension 0, may hold values from 0 to 64, as said below
- remote_source: int32 [32, 32], P(('parts', 'branch', 'sub')), parts along dimension 0, may hold values from 0 to 63
- remote_coupling: bfloat16 [32, 32, 64, 64], P(('parts', 'branch', 'sub')), parts along dimension 0, may hold values from -0.375 to 0.375
- top_source: int32 [128, 8], P(('parts', 'branch')), parts along dimension 0, may hold values from 0 to 63
- top_coupling: bfloat16 [128, 8, 64, 64], P(('parts', 'branch')), parts along dimension 0, may hold values from -0.25 to 0.25
Outputs:
- potential: bfloat16 [2048, 64, 128], P(('parts', 'branch', 'sub')), parts along dimension 0
There are 2 independent parts, one for each index of `parts`. A program takes and returns all parts, laid end to end along the dimension named above; each array names one. Nothing has to cross between parts.
Inputs may be any that keep to these rules, and one draw needn't show every extreme that they name: `near_source`: global leaf index of a near partner of leaf b, within 4 leaves of b; in every draw some leaf has partners exactly 4 away on both sides. `local_source`: global index of a partner leaf in the same aligned block of 64 leaves as leaf b. Leaf b uses its first local_count[b] local partners; some leaf uses all 4. `remote_target`: row g is a sending device; slot s goes to device s // 2; the value is the target leaf within that device's 64 leaves, or 64 for an empty slot. In every draw some device receives 2 filled slots from every sender, and some slot is empty. `remote_source`: source leaf within the sending device's 64 leaves. `top_source`: global index of a top box coupled to top box t.
All inputs are finite; a program needn't handle non-finite values.
Results may differ from a plain program's by a relative error of at most 0.0051.
Values may be sent and summed in bfloat16 or wider, within the bound.
A program may use at most 128 MiB of HBM per device.

v0:
```python
import jax
import jax.numpy as jnp
from jax import lax
from jax.sharding import PartitionSpec as P

HALO_LEAVES = 4


highest = lax.Precision.HIGHEST


def with_halo(shard, sides, width):
    for axis, dim in sides:
        size, length = (lax.axis_size(axis), shard.shape[dim])
        up = [(i, (i + 1) % size) for i in range(size - 1)]
        down = [(j, i) for i, j in up]
        last = lax.slice_in_dim(shard, length - width, length, axis=dim)
        leading = lax.slice_in_dim(shard, 0, width, axis=dim)
        before = lax.ppermute(last, axis, up)
        after = lax.ppermute(leading, axis, down)
        shard = jnp.concatenate([before, shard, after], axis=dim)
    return shard


def on_device(
    charges,
    leaf_basis,
    leaf_transfer,
    parent_transfer,
    near_source,
    near_block,
    local_source,
    local_count,
    local_coupling,
    remote_target,
    remote_source,
    remote_coupling,
    top_source,
    top_coupling,
):
    box_count = charges.shape[0]
    vectors = charges.shape[2]
    rank_width = leaf_basis.shape[2]
    parents = box_count // 4
    sub_size = lax.axis_size("sub")
    device = lax.axis_index("branch") * sub_size + lax.axis_index("sub")
    first_leaf = device * box_count
    leaf_coeffs = jnp.einsum(
        "blr,blv->brv", leaf_basis, charges, preferred_element_type=jnp.float32
    ).astype(jnp.bfloat16)
    lift_mats = leaf_transfer.reshape(parents, 4, rank_width, rank_width)
    parent_coeffs = jnp.einsum(
        "pcrq,pcrv->pqv",
        lift_mats,
        leaf_coeffs.reshape(parents, 4, rank_width, vectors),
        preferred_element_type=jnp.float32,
    )
    lifted = jnp.einsum(
        "prq,prv->pqv", parent_transfer.astype(jnp.float32), parent_coeffs, precision=highest
    )
    branch_tops = lax.psum(lifted, "sub").astype(jnp.bfloat16)
    every_top = lax.all_gather(branch_tops, "branch", axis=0, tiled=True)
    top_field = jnp.einsum(
        "tkrq,tkqv->trv", top_coupling, every_top[top_source], preferred_element_type=jnp.float32
    ).astype(jnp.bfloat16)
    parent_field = jnp.einsum(
        "prq,pqv->prv", parent_transfer, top_field, preferred_element_type=jnp.float32
    )
    lowered = jnp.einsum(
        "pcrq,pqv->pcrv", lift_mats.astype(jnp.float32), parent_field, precision=highest
    ).reshape(box_count, rank_width, vectors)
    outgoing = jnp.einsum(
        "srq,sqv->srv",
        remote_coupling[0],
        leaf_coeffs[remote_source[0]],
        preferred_element_type=jnp.float32,
    ).astype(jnp.bfloat16)
    targets = remote_target[0]
    arrived, labels = (
        lax.all_to_all(outgoing, ("branch", "sub"), split_axis=0, concat_axis=0, tiled=True),
        lax.all_to_all(targets, ("branch", "sub"), split_axis=0, concat_axis=0, tiled=True),
    )
    placing = (labels[None, :] == jnp.arange(box_count, dtype=jnp.int32)[:, None]).astype(
        jnp.bfloat16
    )
    remote_field = jnp.einsum("bs,srv->brv", placing, arrived, preferred_element_type=jnp.float32)
    positions = jnp.arange(local_source.shape[1], dtype=jnp.int32)
    pair_mask = (positions[None, :] < local_count[:, None]).astype(jnp.bfloat16)
    gathered = leaf_coeffs[local_source - first_leaf] * pair_mask[:, :, None, None]
    local_field = jnp.einsum(
        "bkrq,bkqv->brv", local_coupling, gathered, preferred_element_type=jnp.float32
    )
    padded = with_halo(charges, ((("branch", "sub"), 0),), HALO_LEAVES)
    near_values = padded[near_source - first_leaf + HALO_LEAVES]
    near_field = jnp.einsum(
        "bkij,bkjv->biv", near_block, near_values, preferred_element_type=jnp.float32
    )
    leaf_field = (lowered + local_field + remote_field).astype(jnp.bfloat16)
    far_field = jnp.einsum(
        "blr,brv->blv", leaf_basis, leaf_field, preferred_element_type=jnp.float32
    )
    return (far_field + near_field).astype(jnp.bfloat16)


def solution(mesh):
    in_specs = (
        P(("parts", "branch", "sub"), None, None),
        P(("parts", "branch", "sub"), None, None),
        P(("parts", "branch", "sub"), None, None),
        P(("parts", "branch", "sub"), None, None),
        P(("parts", "branch", "sub"), None),
        P(("parts", "branch", "sub"), None, None, None),
        P(("parts", "branch", "sub"), None),
        P(("parts", "branch", "sub")),
        P(("parts", "branch", "sub"), None, None, None),
        P(("parts", "branch", "sub"), None),
        P(("parts", "branch", "sub"), None),
        P(("parts", "branch", "sub"), None, None, None),
        P(("parts", "branch"), None),
        P(("parts", "branch"), None, None, None),
    )
    out_specs = P(("parts", "branch", "sub"), None, None)
    return jax.shard_map(
        on_device, mesh=mesh, in_specs=in_specs, out_specs=out_specs, check_vma=False
    )
```

profile of v0, /device:TPU:0, one launch (start us, length us, event | category | flops | bytes accessed | tf_op | source)
XLA Modules:
  0.0 115.7 jit_solution(8904715686902725253)
XLA Ops:
  6.5 0.5 broadcast.51
  7.0 1.4 %reduce.6 = s32[32]{0:T(128)S(1)} reduce(s32[1,32]{1,0:T(1,128)} %param.23, s32[]{:T(128)} %broadcast.51), dimensions={0}, to_apply=%param.23.reduce_sub_computation.3 | reduce | bytes 260 | tf_op args[9]
  8.4 0.7 all_to_all.9
  9.1 7.4 %all-to-all-start = ((s32[16,2,1]{1,2,0:T(1,128)}), s32[16,2,1]{1,2,0:T(1,128)S(1)}, u32[]{:S(2)}, u32[]{:S(2)}) async-start(s32[16,2,1]{1,2,0:T(1,128)} %bitcast.16), calls=%async_computation | async-start | bytes 16384 | tf_op jit(solution)/shard_map/all_to_all | solution.py:81
  16.5 1.6 %fusion.19 = (bf16[4,64,128]{2,1,0:T(8,128)(2,1)}, bf16[4,64,128]{2,1,0:T(8,128)(2,1)}) fusion(bf16[64,64,128]{2,1,0:T(8,128)(2,1)} %param.14), kind=kLoop, calls=%fused_computation.39 | loop fusion | bytes 262144 | tf_op jit(solution)/shard_map/slice | solution.py:17
  18.1 2.3 %collective-permute-start = (bf16[4,64,128]{2,1,0:T(8,128)(2,1)}, bf16[4,64,128]{2,1,0:T(8,128)(2,1)S(1)}, u32[]{:S(2)}, u32[]{:S(2)}) collective-permute-start(bf16[4,64,128]{2,1,0:T(8,128)(2,1)} %get-tuple-element.5), channel_id=1, source_target_pairs={{0,1},{1,2},{2,3},{3,4},{4,5},{5,6},{6,7},{7,8},{8,9},{9,10},{10,1... | collective-permute-start | bytes 196616 | tf_op jit(solution)/shard_map/ppermute | solution.py:19
  20.4 1.3 %collective-permute-start.1 = (bf16[4,64,128]{2,1,0:T(8,128)(2,1)}, bf16[4,64,128]{2,1,0:T(8,128)(2,1)}, u32[]{:S(2)}, u32[]{:S(2)}) collective-permute-start(bf16[4,64,128]{2,1,0:T(8,128)(2,1)} %get-tuple-element.6), channel_id=1, source_target_pairs={{1,0},{2,1},{3,2},{4,3},{5,4},{6,5},{7,6},{8,7},{9,8},{10,9},{11,1... | collective-permute-start | bytes 196616 | tf_op jit(solution)/shard_map/ppermute | solution.py:20
  21.7 2.1 %convolution_convert_fusion = bf16[64,64,128]{2,1,0:T(8,128)(2,1)S(1)} fusion(bf16[64,64,64]{2,1,0:T(8,128)(2,1)} %param.15, bf16[64,64,128]{2,1,0:T(8,128)(2,1)} %param.14), kind=kOutput, calls=%fused_computation.12 | convolution fusion | flops 67633152 | bytes 2621440 | tf_op jit(solution)/shard_map/blr,blv->brv/dot_general | solution.py:48
  23.8 0.5 convolution_bitcast_fusion.1
  24.3 0.4 copy-done.5
  24.7 1.2 %convolution_bitcast_fusion.3 = f32[16,64,128]{2,1,0:T(8,128)} fusion(f32[16,128,64]{1,2,0:T(8,128)S(1)} %convolution_bitcast_fusion.1, bf16[16,64,64]{2,1,0:T(8,128)(2,1)S(1)} %copy-done.5), kind=kOutput, calls=%fused_computation.18 | convolution fusion | flops 100663296 | bytes 1179648 | tf_op jit(solution)/shard_map/prq,prv->pqv/dot_general | solution.py:58
  26.0 20.7 %all-reduce.1 = bf16[16,64,128]{2,1,0:T(8,128)(2,1)} all-reduce(f32[16,64,128]{2,1,0:T(8,128)} %convolution_bitcast_fusion.3), channel_id=1, replica_groups=mesh['parts'=2,'branch'=4,'sub'=4] {'sub'}, use_global_device_ids=true, to_apply=%region_0.0 | all-reduce | flops 131072 | bytes 786432 | tf_op jit(solution)/shard_map/psum | solution.py:61
  46.8 1.4 %gather_fusion.2 = bf16[32,64,128]{2,1,0:T(8,128)(2,1)} fusion(bf16[64,64,128]{2,1,0:T(8,128)(2,1)S(1)} %convolution_convert_fusion, s32[1024]{0:T(1024)S(1)} %pad_clamp_fusion.1), kind=kCustom, calls=%fused_computation.2 | custom fusion | bytes 1048704 | tf_op jit(solution)/shard_map/gather | solution.py:75
  48.2 2.3 %fusion.9 = bf16[32,64,128]{2,1,0:T(8,128)(2,1)} fusion(bf16[32,64,128]{2,1,0:T(8,128)(2,1)} %gather_fusion.2, bf16[1,32,64,64]{3,2,1,0:T(8,128)(2,1)} %param.25), kind=kOutput, calls=%fused_computation.19 | convolution fusion | flops 33816576 | bytes 1310720 | tf_op jit(solution)/shard_map/srq,sqv->srv/dot_general | solution.py:72
  50.5 4.9 %all-to-all-start.1 = ((bf16[32,64,128]{2,1,0:T(8,128)(2,1)}), bf16[32,64,128]{2,1,0:T(8,128)(2,1)}, u32[]{:S(2)}, u32[]{:S(2)}) async-start(bf16[32,64,128]{2,1,0:T(8,128)(2,1)} %fusion.9), calls=%async_computation.1 | async-start | bytes 1048576 | tf_op jit(solution)/shard_map/all_to_all | solution.py:80
  55.8 0.1 copy.27
  55.9 0.1 reshape.77
  56.0 3.1 %gather_fusion.1 = bf16[256,64,128]{2,1,0:T(8,128)(2,1)} fusion(bf16[64,64,128]{2,1,0:T(8,128)(2,1)S(1)} %convolution_convert_fusion, s32[1024]{0:T(1024)S(1)} %pad_clamp_fusion.2), kind=kCustom, calls=%fused_computation.1 | custom fusion | bytes 8389632 | tf_op jit(solution)/shard_map/gather | solution.py:89
  59.1 0.7 fusion.14
  59.8 0.6 reduce.7
  60.4 0.6 copy-done.7
  61.1 1.4 %pad_maximum_fusion = bf16[72,64,128]{2,1,0:T(8,128)(2,1)S(1)} fusion(bf16[4,64,128]{2,1,0:T(8,128)(2,1)} %collective-permute-done.1, bf16[64,64,128]{2,1,0:T(8,128)(2,1)} %param.14, bf16[4,64,128]{2,1,0:T(8,128)(2,1)} %copy-done.7), kind=kLoop, calls=%fused_computation.21 | loop fusion | flops 1179648 | bytes 2359296 | tf_op jit(solution)/shard_map/concatenate | solution.py:21
  62.5 13.5 %gather_fusion.3 = bf16[512,64,128]{2,1,0:T(8,128)(2,1)} fusion(bf16[72,64,128]{2,1,0:T(8,128)(2,1)S(1)} %pad_maximum_fusion, s32[1024]{0:T(1024)S(1)} %pad_clamp_fusion), kind=kCustom, calls=%fused_computation.3 | custom fusion | bytes 16779264 | tf_op jit(solution)/shard_map/gather | solution.py:94
  76.0 2.3 %all-to-all-done.1 = bf16[32,64,128]{2,1,0:T(8,128)(2,1)} async-done(((bf16[32,64,128]{2,1,0:T(8,128)(2,1)}), bf16[32,64,128]{2,1,0:T(8,128)(2,1)}, u32[]{:S(2)}, u32[]{:S(2)}) %all-to-all-start.1) | async-done | bytes 524320 | tf_op jit(solution)/shard_map/all_to_all | solution.py:80
  78.3 2.9 %fusion.12 = f32[64,64,128]{2,0,1:T(8,128)} fusion(bf16[32,64,128]{2,1,0:T(8,128)(2,1)} %all-to-all-done.1, s32[32]{0:T(128)S(1)} %eq.15), kind=kOutput, calls=%fused_computation.23 | convolution fusion | flops 33556480 | bytes 2621568 | tf_op jit(solution)/shard_map/bs,srv->brv/dot_general | solution.py:86
  81.2 5.6 %all-gather.2.cloned.1.call-done = bf16[64,64,128]{2,1,0:T(8,128)(2,1)} async-done(((bf16[16,64,128]{2,1,0:T(8,128)(2,1)}), bf16[64,64,128]{2,1,0:T(8,128)(2,1)}) %all-gather.2.cloned.1.call-update) | async-done | bytes 1048592 | tf_op jit(solution)/shard_map/all_gather | solution.py:62
  86.8 3.3 %gather_fusion = bf16[128,64,128]{2,1,0:T(8,128)(2,1)} fusion(bf16[64,64,128]{2,1,0:T(8,128)(2,1)} %all-gather.2.cloned.1.call-done, s32[1024]{0:T(1024)S(1)} %pad_clamp_fusion.3), kind=kCustom, calls=%fused_computation | custom fusion | bytes 4194816 | tf_op jit(solution)/shard_map/gather | solution.py:64
  90.1 3.2 %convolution_bitcast_fusion.2 = f32[16,128,64,1]{1,2,3,0:T(8,128)} fusion(bf16[16,64,64]{2,1,0:T(8,128)(2,1)S(1)} %copy-done.5, bf16[16,8,64,64]{3,2,1,0:T(8,128)(2,1)S(1)} %copy-done, bf16[16,8,64,128]{3,2,1,0:T(8,128)(2,1)} %bitcast.79), kind=kOutput, calls=%fused_computation.17 | convolution fusion | flops 151126016 | bytes 3801088 | tf_op jit(solution)/shard_map/prq,pqv->prv/dot_general | solution.py:66
  93.3 2.2 %fusion.20 = f32[16,128,4,64]{1,3,2,0:T(8,128)S(1)} fusion(f32[16,128,64,1]{1,2,3,0:T(8,128)} %convolution_bitcast_fusion.2, bf16[16,4,64,64]{3,2,1,0:T(8,128)(2,1)S(1)} %bitcast.81), kind=kOutput, calls=%fused_computation.40 | convolution fusion | flops 402653184 | bytes 3145728 | tf_op jit(solution)/shard_map/pcrq,pqv->pcrv/dot_general | solution.py:69
  95.6 6.2 %fusion.3 = bf16[64,64,128]{2,1,0:T(8,128)(2,1)S(1)} fusion(f32[16,128,4,64]{1,3,2,0:T(8,128)S(1)} %fusion.20, f32[64,64,128]{2,0,1:T(8,128)S(1)} %copy-done.1, bf16[64,4,64,64]{3,2,1,0:T(8,128)(2,1)} %param.22, bf16[64,4,64,128]{3,2,1,0:T(8,128)(2,1)} %bitcast.78, bf16[64,4]{1,0:T(8,128)(2,1)S(1)} %copy-done.6), kind=kOutput, calls=%fused_computation.8 | convolution fusion | flops 278396928 | bytes 11534848 | tf_op jit(solution)/shard_map/bkrq,bkqv->brv/dot_general | solution.py:90
  101.8 0.4 fusion.21
  102.2 6.6 %fusion.6 = bf16[64,64,128]{2,1,0:T(8,128)(2,1)} fusion(f32[64,128,64]{1,2,0:T(8,128)S(1)} %fusion.21, bf16[64,8,64,64]{3,2,1,0:T(8,128)(2,1)} %param.19, bf16[64,8,64,128]{3,2,1,0:T(8,128)(2,1)S(1)} %bitcast.76), kind=kOutput, calls=%fused_computation.13 | convolution fusion | flops 537919488 | bytes 15728640 | tf_op jit(solution)/shard_map/bkij,bkjv->biv/dot_general | solution.py:95
  (47 shorter events, 0.6 us)
Async XLA Ops:
  6.5 83.6 %copy-start = (bf16[16,8,64,64]{3,2,1,0:T(8,128)(2,1)S(1)}, bf16[16,8,64,64]{3,2,1,0:T(8,128)(2,1)}, u32[]{:S(2)}) copy-start(bf16[16,8,64,64]{3,2,1,0:T(8,128)(2,1)} %param.27) | copy-start | bytes 3145732
  9.1 41.4 %all-to-all-start = ((s32[16,2,1]{1,2,0:T(1,128)}), s32[16,2,1]{1,2,0:T(1,128)S(1)}, u32[]{:S(2)}, u32[]{:S(2)}) async-start(s32[16,2,1]{1,2,0:T(1,128)} %bitcast.16), calls=%async_computation | async-start | bytes 16384 | tf_op jit(solution)/shard_map/all_to_all | solution.py:81
  16.4 70.3 %all-gather.2.cloned.1.call-start = ((), (), s32[]{:S(2)}) async-start(), calls=%async_computation.2 | async-start | bytes 1310720 | tf_op jit(solution)/shard_map/all_gather | solution.py:62
  16.5 7.3 %copy-start.2 = (bf16[64,64,64]{2,1,0:T(8,128)(2,1)S(1)}, bf16[64,64,64]{2,1,0:T(8,128)(2,1)}, u32[]{:S(2)}) copy-start(bf16[64,64,64]{2,1,0:T(8,128)(2,1)} %param.16) | copy-start | bytes 1572868
  18.1 42.3 %collective-permute-start = (bf16[4,64,128]{2,1,0:T(8,128)(2,1)}, bf16[4,64,128]{2,1,0:T(8,128)(2,1)S(1)}, u32[]{:S(2)}, u32[]{:S(2)}) collective-permute-start(bf16[4,64,128]{2,1,0:T(8,128)(2,1)} %get-tuple-element.5), channel_id=1, source_target_pairs={{0,1},{1,2},{2,3},{3,4},{4,5},{5,6},{6,7},{7,8},{8,9},{9,10},{10,1... | collective-permute-start | bytes 196616 | tf_op jit(solution)/shard_map/ppermute | solution.py:19
  20.4 40.6 %collective-permute-start.1 = (bf16[4,64,128]{2,1,0:T(8,128)(2,1)}, bf16[4,64,128]{2,1,0:T(8,128)(2,1)}, u32[]{:S(2)}, u32[]{:S(2)}) collective-permute-start(bf16[4,64,128]{2,1,0:T(8,128)(2,1)} %get-tuple-element.6), channel_id=1, source_target_pairs={{1,0},{2,1},{3,2},{4,3},{5,4},{6,5},{7,6},{8,7},{9,8},{10,9},{11,1... | collective-permute-start | bytes 196616 | tf_op jit(solution)/shard_map/ppermute | solution.py:20
  23.8 1.0 copy-start.5
  23.8 22.9 %copy-start.12 = (s32[1,32]{1,0:T(1,128)S(1)}, s32[1,32]{1,0:T(1,128)}, u32[]{:S(2)}) copy-start(s32[1,32]{1,0:T(1,128)} %param.24) | copy-start | bytes 388
  26.0 24.5 %copy-start.8 = (s32[16,8]{0,1:T(8,128)S(1)}, s32[16,8]{0,1:T(8,128)}, u32[]{:S(2)}) copy-start(s32[16,8]{0,1:T(8,128)} %param.26) | copy-start | bytes 1540
  46.7 8.7 %copy-start.9 = (s32[64,8]{0,1:T(8,128)S(1)}, s32[64,8]{0,1:T(8,128)}, u32[]{:S(2)}) copy-start(s32[64,8]{0,1:T(8,128)} %param.18) | copy-start | bytes 6148
  46.7 9.1 %copy-start.10 = (s32[64,4]{0,1:T(4,128)S(1)}, s32[64,4]{0,1:T(4,128)}, u32[]{:S(2)}) copy-start(s32[64,4]{0,1:T(4,128)} %param.20) | copy-start | bytes 3076
  50.5 27.8 %all-to-all-start.1 = ((bf16[32,64,128]{2,1,0:T(8,128)(2,1)}), bf16[32,64,128]{2,1,0:T(8,128)(2,1)}, u32[]{:S(2)}, u32[]{:S(2)}) async-start(bf16[32,64,128]{2,1,0:T(8,128)(2,1)} %fusion.9), calls=%async_computation.1 | async-start | bytes 1048576 | tf_op jit(solution)/shard_map/all_to_all | solution.py:80
  56.0 3.1 %copy-start.11 = (s32[64]{0:T(128)S(1)}, s32[64]{0:T(128)}, u32[]{:S(2)}) copy-start(s32[64]{0:T(128)} %param.21) | copy-start | bytes 772
  60.4 0.6 copy-start.7
  90.1 3.2 %copy-start.3 = (bf16[64,64,64]{2,1,0:T(8,128)(2,1)S(1)}, bf16[64,64,64]{2,1,0:T(8,128)(2,1)}, u32[]{:S(2)}) copy-start(bf16[64,64,64]{2,1,0:T(8,128)(2,1)} %param.16) | copy-start | bytes 1572868
  93.3 2.2 %copy-start.1 = (f32[64,64,128]{2,0,1:T(8,128)S(1)}, f32[64,64,128]{2,0,1:T(8,128)}, u32[]{:S(2)}) copy-start(f32[64,64,128]{2,0,1:T(8,128)} %fusion.12) | copy-start | bytes 6291460
  93.3 2.2 %copy-start.6 = (bf16[64,4]{1,0:T(8,128)(2,1)S(1)}, bf16[64,4]{1,0:T(8,128)(2,1)}, u32[]{:S(2)}) copy-start(bf16[64,4]{1,0:T(8,128)(2,1)} %fusion.14) | copy-start | bytes 1540
  95.5 6.7 %slice-start = ((s8[8388608]{0:T(1024)(128)(4,1)}), s8[4194304]{0:T(1024)(128)(4,1)S(1)}, s32[]{:S(2)}) async-start(s8[8388608]{0:T(1024)(128)(4,1)} %bitcast.74), calls=%async_computation.3 | async-start | bytes 8388608
  95.5 6.2 %copy-start.4 = (bf16[64,64,64]{2,1,0:T(8,128)(2,1)S(1)}, bf16[64,64,64]{2,1,0:T(8,128)(2,1)}, u32[]{:S(2)}) copy-start(bf16[64,64,64]{2,1,0:T(8,128)(2,1)} %param.15) | copy-start | bytes 1572868
  95.5 6.7 %slice-start.1 = ((s8[8388608]{0:T(1024)(128)(4,1)}), s8[4194304]{0:T(1024)(128)(4,1)S(1)}, s32[]{:S(2)}) async-start(s8[8388608]{0:T(1024)(128)(4,1)} %bitcast.74), calls=%async_computation.4 | async-start | bytes 8388608
Sparse Core Ops, SparseCore 0:
  46.8 39.8 all-gather.1
where the time goes:
time: 116 us
  matrix products  27.6 us (24%)
  local copies, waits for them, and re-layouts  25.9 us (22%)
  blocking collectives  20.7 us (18%)
  starting transfers between devices  15.9 us (14%)
  between operations  13.7 us (12%)
  waiting for transfers between devices  7.84 us (7%)
  other arithmetic  4.07 us (4%)
    psum x1, blocking collectives, on_device(): branch_tops = lax.psum(lifted, 'sub').astype(jnp.bfloat16)  20.7 us
    gather x1, local copies, waits for them, and re-layouts, on_device(): near_values = padded[near_source - first_leaf + HALO_LEAVES]  13.5 us
    all_to_all x1, starting transfers between devices, on_device(): lax.all_to_all(targets, ('branch', 'sub'), split_axis=0, concat_axis=0, t...  7.36 us
    dot_general x1, matrix products, on_device(): jnp.einsum('bkij,bkjv->biv', near_block, near_values, preferred_element_t...  6.63 us
    dot_general x1, matrix products, on_device(): jnp.einsum('bkrq,bkqv->brv', local_coupling, gathered, preferred_element_...  6.19 us
    all_gather x1, waiting for transfers between devices, on_device(): every_top = lax.all_gather(branch_tops, 'branch', axis=0, tiled=True)  5.55 us
    all_to_all x1, starting transfers between devices, on_device(): lax.all_to_all(outgoing, ('branch', 'sub'), split_axis=0, concat_axis=0,...  4.89 us
    gather x1, local copies, waits for them, and re-layouts, on_device(): every_top[top_source]  3.34 us
  transfers between devices with their start and end apart: 5, of which 2 were waited for; matrix products, arithmetic and copies ran while one was open for 28% of the time, Pallas kernels for 0%

commit v1 on v0

v1 whole, which is shorter than its diff:
```python
import functools

import jax
import jax.numpy as jnp
from jax import lax
from jax.experimental import pallas as pl
from jax.experimental.pallas import tpu as pltpu
from jax.sharding import PartitionSpec as P

HALO_LEAVES = 4
CAPACITY = 2
MESH = pl.DeviceIdType.MESH
F32 = jnp.float32
BF16 = jnp.bfloat16


def side_by_side(mats, values):
    return jnp.dot(
        jnp.concatenate(mats, axis=1),
        jnp.concatenate(values, axis=0),
        preferred_element_type=F32,
    )


def across(mat, value):
    return lax.dot_general(mat, value, (((0,), (0,)), ((), ())), preferred_element_type=F32)


def loop(start, stop, unroll, compute, store):
    assert (stop - start) % unroll == 0

    def body(step, carry):
        first = start + step * unroll
        results = [compute(first + i) for i in range(unroll)]
        for i, result in enumerate(results):
            store(first + i, result)
        return carry

    lax.fori_loop(0, (stop - start) // unroll, body, 0)


def kernel(
    branch_size,
    sub_size,
    near_src,
    local_src,
    local_cnt,
    remote_src,
    top_src,
    remote_tgt,
    charges_hbm,
    basis_hbm,
    transfer_hbm,
    raise_hbm,
    near_hbm,
    local_hbm,
    remote_hbm,
    top_hbm,
    out_hbm,
    padded,
    basis,
    transfer,
    raises,
    near,
    local,
    remote,
    top,
    coeffs,
    near_field,
    local_field,
    outgoing,
    arrived,
    chain,
    parent,
    lifted,
    partial,
    partials,
    tops,
    field,
    leaf_field,
    result,
    label_tile,
    labels,
    prev_vec,
    last_vec,
    prev_idx,
    last_idx,
    load_sem,
    out_sem,
    idx_sem,
    halo_send,
    halo_recv,
    label_send,
    label_recv,
    slot_send,
    slot_recv,
    part_send,
    part_recv,
    up_send,
    up_recv,
    far_send,
    far_recv,
    twin_send,
    twin_recv,
):
    parts = lax.axis_index("parts")
    branch = lax.axis_index("branch")
    sub = lax.axis_index("sub")
    devices = branch_size * sub_size
    me = branch * sub_size + sub
    boxes = basis.shape[0]
    rank, vectors = coeffs.shape[1:]
    assert sub_size == 4 and boxes & (boxes - 1) == 0
    slots = devices * CAPACITY
    parents = boxes // 4
    owned = parents // sub_size
    near_count, local_room, top_pairs = near.shape[1], local.shape[1], top.shape[1]
    before = me * boxes - HALO_LEAVES

    def at(peer):
        return (parts, lax.div(peer, sub_size), lax.rem(peer, sub_size))

    def peer_of(i):
        return lax.rem(me + i, devices)

    loads = [
        (charges_hbm, padded.at[pl.ds(HALO_LEAVES, boxes)]),
        (basis_hbm, basis),
        (transfer_hbm, transfer),
        (raise_hbm, raises),
        (remote_hbm.at[0], remote),
        (local_hbm, local),
        (near_hbm, near),
        (top_hbm, top),
    ]
    loads = [pltpu.make_async_copy(a, b, load_sem.at[i]) for i, (a, b) in enumerate(loads)]
    for load in loads:
        load.start()

    barrier = pltpu.get_barrier_semaphore()

    def greet(i, carry):
        pl.semaphore_signal(barrier, inc=1, device_id=at(peer_of(i)), device_id_type=MESH)
        return carry

    lax.fori_loop(1, devices, greet, 0)
    label_tile[...] = jnp.broadcast_to(remote_tgt[...], label_tile.shape)
    pl.semaphore_wait(barrier, devices - 1)

    halo_up = pltpu.make_async_remote_copy(
        src_ref=charges_hbm.at[pl.ds(boxes - HALO_LEAVES, HALO_LEAVES)],
        dst_ref=padded.at[pl.ds(0, HALO_LEAVES)],
        send_sem=halo_send.at[0],
        recv_sem=halo_recv.at[0],
        device_id=at(peer_of(1)),
        device_id_type=MESH,
    )
    halo_down = pltpu.make_async_remote_copy(
        src_ref=charges_hbm.at[pl.ds(0, HALO_LEAVES)],
        dst_ref=padded.at[pl.ds(HALO_LEAVES + boxes, HALO_LEAVES)],
        send_sem=halo_send.at[1],
        recv_sem=halo_recv.at[1],
        device_id=at(peer_of(devices - 1)),
        device_id_type=MESH,
    )
    halo_up.start()
    halo_down.start()

    def label_copy(peer, slot):
        return pltpu.make_async_remote_copy(
            src_ref=label_tile,
            dst_ref=labels.at[slot],
            send_sem=label_send.at[peer],
            recv_sem=label_recv.at[slot],
            device_id=at(peer),
            device_id_type=MESH,
        )

    def send_label(i, carry):
        label_copy(peer_of(i), me).start()
        return carry

    lax.fori_loop(1, devices, send_label, 0)
    labels[me] = label_tile[...]

    loads[0].wait()
    loads[1].wait()

    def put_coeffs(b, value):
        coeffs[b] = value.astype(BF16)

    loop(0, boxes, 8, lambda b: across(basis[b], padded[HALO_LEAVES + b]), put_coeffs)
    coeffs[boxes] = jnp.zeros((rank, vectors), BF16)
    loads[2].wait()
    loads[3].wait()

    def put_parent(p, value):
        parent[p] = value.astype(BF16)

    def lift(p):
        four = pl.ds(pl.multiple_of(p * 4, 4), 4)
        return across(
            transfer[four].reshape(4 * rank, rank), coeffs[four].reshape(4 * rank, vectors)
        )

    loop(0, parents, 4, lift, put_parent)

    def put_lifted(p, value):
        lifted[p] = value
        partial[p] = value.astype(BF16)

    loop(0, parents, 4, lambda p: across(raises[p], parent[p]), put_lifted)

    def part_copy(other, slot):
        return pltpu.make_async_remote_copy(
            src_ref=partial.at[pl.ds(other * owned, owned)],
            dst_ref=partials.at[slot],
            send_sem=part_send.at[other],
            recv_sem=part_recv.at[slot],
            device_id=(parts, branch, other),
            device_id_type=MESH,
        )

    for i in range(1, sub_size):
        part_copy(lax.rem(sub + i, sub_size), sub).start()

    loads[4].wait()

    def contribution(s):
        return jnp.dot(remote[s], coeffs[remote_src[0, s]], preferred_element_type=F32)

    def put_outgoing(s, value):
        outgoing[lax.div(s, CAPACITY), lax.rem(s, CAPACITY)] = value.astype(BF16)

    loop(0, slots, 8, contribution, put_outgoing)

    def slot_copy(peer, slot):
        return pltpu.make_async_remote_copy(
            src_ref=outgoing.at[peer],
            dst_ref=arrived.at[slot],
            send_sem=slot_send.at[peer],
            recv_sem=slot_recv.at[slot],
            device_id=at(peer),
            device_id_type=MESH,
        )

    def send_slots(i, carry):
        slot_copy(peer_of(i), me).start()
        return carry

    lax.fori_loop(1, devices, send_slots, 0)
    arrived[me] = outgoing[me]

    def local_product(b):
        used = local_cnt[b]
        chosen = [
            coeffs[jnp.where(k < used, local_src[b, k] & (boxes - 1), boxes)]
            for k in range(local_room)
        ]
        return side_by_side([local[b, k] for k in range(local_room)], chosen)

    def put_local(b, value):
        local_field[b] = value

    def near_product(b):
        chosen = [
            padded[jnp.clip(near_src[b, k] - before, 0, boxes + 2 * HALO_LEAVES - 1)]
            for k in range(near_count)
        ]
        return side_by_side([near[b, k] for k in range(near_count)], chosen)

    def put_near(b, value):
        near_field[b] = value

    quarter = boxes // 4
    loads[5].wait()
    loop(0, boxes // 2, 2, local_product, put_local)

    for i in range(1, sub_size):
        part_copy(sub, lax.rem(sub + i, sub_size)).wait_recv()
    for j in range(owned):
        total = lifted[sub * owned + j]
        for i in range(1, sub_size):
            total += partials[lax.rem(sub + i, sub_size), j].astype(F32)
        tops[branch, sub, j] = total.astype(BF16)

    far_sub = sub + sub_size // 2 - (sub // (sub_size // 2)) * sub_size
    twin_sub = sub + 1 - 2 * lax.rem(sub, 2)
    twin_far = far_sub + 1 - 2 * lax.rem(far_sub, 2)

    def top_copy(owner_branch, owner_sub, send_sem, recv_sem, target):
        block = tops.at[owner_branch, owner_sub]
        return pltpu.make_async_remote_copy(
            src_ref=block,
            dst_ref=block,
            send_sem=send_sem,
            recv_sem=recv_sem,
            device_id=target,
            device_id_type=MESH,
        )

    def up_copy(other, owner):
        return top_copy(owner, sub, up_send.at[other], up_recv.at[owner], (parts, other, sub))

    def far_copy(owner, column):
        return top_copy(
            owner, column, far_send.at[owner], far_recv.at[owner], (parts, branch, far_sub)
        )

    def twin_copy(owner, column, which):
        return top_copy(
            owner,
            column,
            twin_send.at[which, owner],
            twin_recv.at[which, owner],
            (parts, branch, twin_sub),
        )

    def other_branch(i):
        return lax.rem(branch + i, branch_size)

    def send_up(i, carry):
        up_copy(other_branch(i), branch).start()
        return carry

    def pass_on(i, carry):
        owner = other_branch(i)
        up_copy(branch, owner).wait_recv()
        far_copy(owner, sub).start()
        twin_copy(owner, sub, 0).start()
        return carry

    def pass_twin(i, carry):
        owner = other_branch(i)
        far_copy(owner, far_sub).wait_recv()
        twin_copy(owner, far_sub, 1).start()
        return carry

    def take_twin(i, carry):
        twin_copy(i, twin_sub, 0).wait_recv()
        twin_copy(i, twin_far, 1).wait_recv()
        return carry

    lax.fori_loop(1, branch_size, send_up, 0)
    far_copy(branch, sub).start()
    twin_copy(branch, sub, 0).start()

    loop(boxes // 2, boxes, 2, local_product, put_local)
    loads[6].wait()
    halo_up.wait_recv()
    halo_down.wait_recv()
    loop(0, quarter, 2, near_product, put_near)
    lax.fori_loop(1, branch_size, pass_on, 0)
    loop(quarter, 2 * quarter, 2, near_product, put_near)
    lax.fori_loop(0, branch_size, pass_twin, 0)
    loop(2 * quarter, boxes, 2, near_product, put_near)

    def take_label(i, carry):
        label_copy(me, peer_of(i)).wait_recv()
        return carry

    lax.fori_loop(1, devices, take_label, 0)
    rows = jnp.max(labels[...], axis=1)
    lane = lax.broadcasted_iota(jnp.int32, rows.shape, 1)
    columns = [
        jnp.max(jnp.where(lane == me * CAPACITY + c, rows, -1), axis=1, keepdims=True)
        for c in range(CAPACITY)
    ]
    wide = prev_vec.shape[1]
    slot_lane = lax.broadcasted_iota(jnp.int32, (devices, wide), 1)
    slot_row = lax.broadcasted_iota(jnp.int32, (devices, wide), 0) * CAPACITY
    along = sum(
        jnp.sum(jnp.where(slot_lane == slot_row + c, columns[c], 0), axis=0, keepdims=True)
        for c in range(CAPACITY)
    )
    prev = jnp.full((1, wide), -1, jnp.int32)
    for c in range(CAPACITY):
        same = (columns[c] == along) & (slot_row + c < slot_lane)
        prev = jnp.maximum(
            prev, jnp.max(jnp.where(same, slot_row + c, -1), axis=0, keepdims=True)
        )
    broad = last_vec.shape[1]
    box_lane = lax.broadcasted_iota(jnp.int32, (devices, broad), 1)
    box_row = lax.broadcasted_iota(jnp.int32, (devices, broad), 0) * CAPACITY
    last = jnp.full((1, broad), -1, jnp.int32)
    for c in range(CAPACITY):
        last = jnp.maximum(
            last,
            jnp.max(jnp.where(columns[c] == box_lane, box_row + c, -1), axis=0, keepdims=True),
        )
    prev_vec[...] = jnp.broadcast_to(jnp.where(prev < 0, slots, prev), prev_vec.shape)
    last_vec[...] = jnp.broadcast_to(jnp.where(last < 0, slots, last), last_vec.shape)
    prev_copy = pltpu.make_async_copy(prev_vec, prev_idx, idx_sem.at[0])
    last_copy = pltpu.make_async_copy(last_vec, last_idx, idx_sem.at[1])
    prev_copy.start()
    last_copy.start()

    def take_slots(i, carry):
        slot_copy(me, peer_of(i)).wait_recv()
        return carry

    lax.fori_loop(1, devices, take_slots, 0)
    prev_copy.wait()
    last_copy.wait()
    chain[slots] = jnp.zeros((rank, vectors), F32)

    def link(s, carry):
        value = arrived[lax.div(s, CAPACITY), lax.rem(s, CAPACITY)].astype(F32)
        chain[s] = value + chain[prev_idx[0, s]]
        return carry

    lax.fori_loop(0, slots, link, 0)

    loads[7].wait()
    lax.fori_loop(0, branch_size, take_twin, 0)

    def top_product(t):
        chosen = []
        for k in range(top_pairs):
            source = top_src[t, k]
            owner = lax.div(source, parents)
            inner = lax.rem(source, parents)
            chosen.append(tops[owner, lax.div(inner, owned), lax.rem(inner, owned)])
        return side_by_side([top[t, k] for k in range(top_pairs)], chosen)

    def put_field(t, value):
        field[t] = value.astype(BF16)

    loop(0, parents, 4, top_product, put_field)
    loop(
        0,
        parents,
        8,
        lambda p: jnp.dot(raises[p], field[p], preferred_element_type=F32),
        put_parent,
    )

    def lower(p):
        four = pl.ds(pl.multiple_of(p * 4, 4), 4)
        return jnp.dot(
            transfer[four].reshape(4 * rank, rank), parent[p], preferred_element_type=F32
        )

    def put_leaf(p, value):
        for c in range(4):
            b = p * 4 + c
            whole = value[c * rank : (c + 1) * rank] + local_field[b] + chain[last_idx[0, b]]
            leaf_field[b] = whole.astype(BF16)

    loop(0, parents, 2, lower, put_leaf)

    def potential(b):
        return near_field[b] + jnp.dot(basis[b], leaf_field[b], preferred_element_type=F32)

    def put_result(b, value):
        result[b] = value.astype(BF16)

    stores = []
    for piece in range(4):
        loop(piece * quarter, (piece + 1) * quarter, 8, potential, put_result)
        rows_of = pl.ds(piece * quarter, quarter)
        stores.append(
            pltpu.make_async_copy(result.at[rows_of], out_hbm.at[rows_of], out_sem.at[piece])
        )
        stores[-1].start()

    halo_up.wait_send()
    halo_down.wait_send()

    def sent(i, carry):
        peer = peer_of(i)
        label_copy(peer, me).wait_send()
        slot_copy(peer, me).wait_send()
        return carry

    lax.fori_loop(1, devices, sent, 0)
    for i in range(1, sub_size):
        part_copy(lax.rem(sub + i, sub_size), sub).wait_send()

    def sent_up(i, carry):
        up_copy(other_branch(i), branch).wait_send()
        return carry

    lax.fori_loop(1, branch_size, sent_up, 0)

    def sent_on(i, carry):
        far_copy(i, sub).wait_send()
        twin_copy(i, sub, 0).wait_send()
        twin_copy(i, far_sub, 1).wait_send()
        return carry

    lax.fori_loop(0, branch_size, sent_on, 0)
    for store in stores:
        store.wait()


def on_device(
    charges,
    leaf_basis,
    leaf_transfer,
    parent_transfer,
    near_source,
    near_block,
    local_source,
    local_count,
    local_coupling,
    remote_target,
    remote_source,
    remote_coupling,
    top_source,
    top_coupling,
):
    boxes, points, vectors = charges.shape
    rank = leaf_basis.shape[2]
    branch_size, sub_size = lax.axis_size("branch"), lax.axis_size("sub")
    devices = branch_size * sub_size
    slots = remote_target.shape[1]
    parents = parent_transfer.shape[0]
    owned = parents // sub_size
    wide = -(-slots // 128) * 128
    broad = -(-boxes // 128) * 128
    vmem = pltpu.VMEM
    dma = pltpu.SemaphoreType.DMA
    scratch = [
        vmem((boxes + 2 * HALO_LEAVES, points, vectors), BF16),
        vmem(leaf_basis.shape, BF16),
        vmem(leaf_transfer.shape, BF16),
        vmem(parent_transfer.shape, BF16),
        vmem(near_block.shape, BF16),
        vmem(local_coupling.shape, BF16),
        vmem(remote_coupling.shape[1:], BF16),
        vmem(top_coupling.shape, BF16),
        vmem((boxes + 1, rank, vectors), BF16),
        vmem((boxes, points, vectors), F32),
        vmem((boxes, rank, vectors), F32),
        vmem((devices, CAPACITY, rank, vectors), BF16),
        vmem((devices, CAPACITY, rank, vectors), BF16),
        vmem((slots + 1, rank, vectors), F32),
        vmem((parents, rank, vectors), BF16),
        vmem((parents, rank, vectors), F32),
        vmem((parents, rank, vectors), BF16),
        vmem((sub_size, owned, rank, vectors), BF16),
        vmem((branch_size, sub_size, owned, rank, vectors), BF16),
        vmem((parents, rank, vectors), BF16),
        vmem((boxes, rank, vectors), BF16),
        vmem((boxes, points, vectors), BF16),
        vmem((8, slots), jnp.int32),
        vmem((devices, 8, slots), jnp.int32),
        vmem((8, wide), jnp.int32),
        vmem((8, broad), jnp.int32),
        pltpu.SMEM((8, wide), jnp.int32),
        pltpu.SMEM((8, broad), jnp.int32),
        dma((8,)),
        dma((4,)),
        dma((2,)),
        dma((2,)),
        dma((2,)),
        dma((devices,)),
        dma((devices,)),
        dma((devices,)),
        dma((devices,)),
        dma((sub_size,)),
        dma((sub_size,)),
        dma((branch_size,)),
        dma((branch_size,)),
        dma((branch_size,)),
        dma((branch_size,)),
        dma((2, branch_size)),
        dma((2, branch_size)),
    ]
    smem = pl.BlockSpec(memory_space=pltpu.SMEM)
    anywhere = pl.BlockSpec(memory_space=pl.ANY)
    return pl.pallas_call(
        functools.partial(kernel, branch_size, sub_size),
        out_shape=jax.ShapeDtypeStruct((boxes, points, vectors), BF16),
        in_specs=[smem] * 5 + [pl.BlockSpec(memory_space=pltpu.VMEM)] + [anywhere] * 8,
        out_specs=anywhere,
        scratch_shapes=scratch,
        compiler_params=pltpu.CompilerParams(
            collective_id=0, has_side_effects=True, vmem_limit_bytes=60 * 2**20
        ),
    )(
        near_source,
        local_source,
        local_count,
        remote_source,
        top_source,
        remote_target,
        charges,
        leaf_basis,
        leaf_transfer,
        parent_transfer,
        near_block,
        local_coupling,
        remote_coupling,
        top_coupling,
    )


def solution(mesh):
    boxed = P(("parts", "branch", "sub"))
    topped = P(("parts", "branch"))
    return jax.shard_map(
        on_device,
        mesh=mesh,
        in_specs=(boxed,) * 12 + (topped, topped),
        out_specs=boxed,
        check_vma=False,
    )
```

time: 116 us -> 52.3 us (0.45)
  Pallas kernels: 0 us -> 45 us
  matrix products: 27.6 us -> 0 us
  blocking collectives: 20.7 us -> 0 us
  local copies, waits for them, and re-layouts: 25.9 us -> 6.36 us
  starting transfers between devices: 15.9 us -> 0 us
  between operations: 13.7 us -> 0.01 us
  waiting for transfers between devices: 7.84 us -> 0 us
  other arithmetic: 4.07 us -> 0 us
    pallas_call x0 -> x1, Pallas kernels: none -> 45 us  [on_device(): pl.pallas_call(functools.partial(kernel, branch_size, sub_size), out_shap...]
    dot_general x10 -> x0, matrix products: 27.6 us -> none  [the longest x1 6.63 us: on_device(): jnp.einsum('bkij,bkjv->biv', near_block, near_values, preferred_element_t...]
    gather x4 -> x0, local copies, waits for them, and re-layouts: 21.3 us -> none  [the longest x1 13.5 us: on_device(): near_values = padded[near_source - first_leaf + HALO_LEAVES]]
    psum x1 -> x0, blocking collectives: 20.7 us -> none  [on_device(): branch_tops = lax.psum(lifted, 'sub').astype(jnp.bfloat16)]
    all_to_all x2 -> x0, starting transfers between devices: 12.2 us -> none  [the longest x1 7.36 us: on_device(): lax.all_to_all(targets, ('branch', 'sub'), split_axis=0, concat_axis=0, t...]
    all_gather x1 -> x0, waiting for transfers between devices: 5.55 us -> none  [on_device(): every_top = lax.all_gather(branch_tops, 'branch', axis=0, tiled=True)]
    unnamed x31 -> x4, local copies, waits for them, and re-layouts: 1.61 us -> 6.36 us
    ppermute x2 -> x0, starting transfers between devices: 3.59 us -> none  [the longest x1 2.3 us: with_halo(): before = lax.ppermute(last, axis, up)]
  transfers between devices with their start and end apart: 5 -> 0, of which waited for: 2 -> 0; matrix products, arithmetic and copies ran while one was open for 28% -> 0% of each run, Pallas kernels for 0% -> 0%
where the time goes in v1:
time: 52.3 us; the launch traced here: 51.4 us
  Pallas kernels  45 us (86%)
  local copies, waits for them, and re-layouts  6.36 us (12%)
    pallas_call x1, Pallas kernels, on_device(): pl.pallas_call(functools.partial(kernel, branch_size, sub_size), out_shap...  45 us
    unnamed x4, local copies, waits for them, and re-layouts  6.36 us

profile of v1, /device:TPU:0, one launch (start us, length us, event | category | flops | bytes accessed | tf_op | source)
XLA Modules:
  0.0 51.4 jit_solution(17435117252716594315)
XLA Ops:
  0.0 1.3 %copy.17.top_src = s32[16,8]{1,0:T(8,128)} copy(s32[16,8]{0,1:T(8,128)} %param.26) | data formatting | bytes 1024 | tf_op args[12]
  1.3 1.4 %copy.15.near_src = s32[64,8]{1,0:T(8,128)} copy(s32[64,8]{0,1:T(8,128)} %param.18) | data formatting | bytes 4096 | tf_op args[4]
  2.7 1.4 %copy.16.local_src = s32[64,4]{1,0:T(8,128)} copy(s32[64,4]{0,1:T(4,128)} %param.20) | data formatting | bytes 2048 | tf_op args[6]
  4.1 45.0 %shard_map.136 = bf16[64,64,128]{2,1,0:T(8,128)(2,1)} custom-call(s32[64,8]{1,0:T(8,128)} %copy.15.near_src, s32[64,4]{1,0:T(8,128)} %copy.16.local_src, s32[64]{0:T(128)} %local_cnt.1, s32[1,32]{1,0:T(1,128)} %remote_src.1, s32[16,8]{1,0:T(8,128)} %copy.17.top_src, s32[1,32]{1,0:T(1,128)} %remote_tgt.1, bf16[64,64,128]{2,1,0:T(8,128)(2,1)} %charges_hbm.1, ...), custom_call_target="tpu_custom_call" | custom-call | tf_op jit(solution)/shard_map/pallas_call | solution.py:573
  49.1 2.3 %copy.19 = bf16[64,64,128]{2,1,0:T(8,128)(2,1)} copy(bf16[64,64,128]{2,1,0:T(8,128)(2,1)} %shard_map.136) | data formatting | bytes 2097152

commit v2 on v1

--- a/solution.py
+++ b/solution.py
@@ -10,6 +10,8 @@
 HALO_LEAVES = 4
 CAPACITY = 2
 MESH = pl.DeviceIdType.MESH
+EARLY = 5
+NU, LU, TU = 8, 16, 8
 F32 = jnp.float32
 BF16 = jnp.bfloat16
 
@@ -42,12 +44,12 @@
 def kernel(
     branch_size,
     sub_size,
-    near_src,
-    local_src,
-    local_cnt,
-    remote_src,
-    top_src,
-    remote_tgt,
+    near_src_hbm,
+    local_src_hbm,
+    local_cnt_hbm,
+    remote_src_hbm,
+    top_src_hbm,
+    remote_tgt_hbm,
     charges_hbm,
     basis_hbm,
     transfer_hbm,
@@ -57,6 +59,12 @@
     remote_hbm,
     top_hbm,
     out_hbm,
+    near_src,
+    local_src,
+    local_cnt,
+    remote_src,
+    top_src,
+    remote_tgt,
     padded,
     basis,
     transfer,
@@ -112,6 +120,7 @@
     rank, vectors = coeffs.shape[1:]
     assert sub_size == 4 and boxes & (boxes - 1) == 0
     slots = devices * CAPACITY
+    early = 1 + (devices - 1) * EARLY // 15
     parents = boxes // 4
     owned = parents // sub_size
     near_count, local_room, top_pairs = near.shape[1], local.shape[1], top.shape[1]
@@ -132,9 +141,15 @@
         (local_hbm, local),
         (near_hbm, near),
         (top_hbm, top),
+        (remote_tgt_hbm, remote_tgt),
+        (remote_src_hbm, remote_src),
+        (local_src_hbm, local_src),
+        (local_cnt_hbm, local_cnt),
+        (near_src_hbm, near_src),
+        (top_src_hbm, top_src),
     ]
     loads = [pltpu.make_async_copy(a, b, load_sem.at[i]) for i, (a, b) in enumerate(loads)]
-    for load in loads:
+    for load in loads[8:] + loads[:5]:
         load.start()
 
     barrier = pltpu.get_barrier_semaphore()
@@ -144,6 +159,7 @@
         return carry
 
     lax.fori_loop(1, devices, greet, 0)
+    loads[8].wait()
     label_tile[...] = jnp.broadcast_to(remote_tgt[...], label_tile.shape)
     pl.semaphore_wait(barrier, devices - 1)
 
@@ -185,6 +201,8 @@
 
     loads[0].wait()
     loads[1].wait()
+    for load in loads[5:8]:
+        load.start()
 
     def put_coeffs(b, value):
         coeffs[b] = value.astype(BF16)
@@ -225,6 +243,7 @@
         part_copy(lax.rem(sub + i, sub_size), sub).start()
 
     loads[4].wait()
+    loads[9].wait()
 
     def contribution(s):
         return jnp.dot(remote[s], coeffs[remote_src[0, s]], preferred_element_type=F32)
@@ -248,13 +267,13 @@
         slot_copy(peer_of(i), me).start()
         return carry
 
-    lax.fori_loop(1, devices, send_slots, 0)
+    lax.fori_loop(1, early, send_slots, 0)
     arrived[me] = outgoing[me]
 
     def local_product(b):
         used = local_cnt[b]
         chosen = [
-            coeffs[jnp.where(k < used, local_src[b, k] & (boxes - 1), boxes)]
+            coeffs[jnp.where(k < used, local_src[k, b] & (boxes - 1), boxes)]
             for k in range(local_room)
         ]
         return side_by_side([local[b, k] for k in range(local_room)], chosen)
@@ -264,7 +283,7 @@
 
     def near_product(b):
         chosen = [
-            padded[jnp.clip(near_src[b, k] - before, 0, boxes + 2 * HALO_LEAVES - 1)]
+            padded[jnp.clip(near_src[k, b] - before, 0, boxes + 2 * HALO_LEAVES - 1)]
             for k in range(near_count)
         ]
         return side_by_side([near[b, k] for k in range(near_count)], chosen)
@@ -274,7 +293,9 @@
 
     quarter = boxes // 4
     loads[5].wait()
-    loop(0, boxes // 2, 2, local_product, put_local)
+    loads[10].wait()
+    loads[11].wait()
+    loop(0, boxes // 2, LU, local_product, put_local)
 
     for i in range(1, sub_size):
         part_copy(sub, lax.rem(sub + i, sub_size)).wait_recv()
@@ -345,15 +366,17 @@
     far_copy(branch, sub).start()
     twin_copy(branch, sub, 0).start()
 
-    loop(boxes // 2, boxes, 2, local_product, put_local)
+    loop(boxes // 2, boxes, LU, local_product, put_local)
     loads[6].wait()
+    loads[12].wait()
     halo_up.wait_recv()
     halo_down.wait_recv()
-    loop(0, quarter, 2, near_product, put_near)
+    loop(0, quarter, NU, near_product, put_near)
     lax.fori_loop(1, branch_size, pass_on, 0)
-    loop(quarter, 2 * quarter, 2, near_product, put_near)
+    lax.fori_loop(early, devices, send_slots, 0)
+    loop(quarter, 2 * quarter, NU, near_product, put_near)
     lax.fori_loop(0, branch_size, pass_twin, 0)
-    loop(2 * quarter, boxes, 2, near_product, put_near)
+    loop(2 * quarter, boxes, NU, near_product, put_near)
 
     def take_label(i, carry):
         label_copy(me, peer_of(i)).wait_recv()
@@ -412,12 +435,13 @@
     lax.fori_loop(0, slots, link, 0)
 
     loads[7].wait()
+    loads[13].wait()
     lax.fori_loop(0, branch_size, take_twin, 0)
 
     def top_product(t):
         chosen = []
         for k in range(top_pairs):
-            source = top_src[t, k]
+            source = top_src[k, t]
             owner = lax.div(source, parents)
             inner = lax.rem(source, parents)
             chosen.append(tops[owner, lax.div(inner, owned), lax.rem(inner, owned)])
@@ -426,7 +450,7 @@
     def put_field(t, value):
         field[t] = value.astype(BF16)
 
-    loop(0, parents, 4, top_product, put_field)
+    loop(0, parents, TU, top_product, put_field)
     loop(
         0,
         parents,
@@ -521,7 +545,14 @@
     broad = -(-boxes // 128) * 128
     vmem = pltpu.VMEM
     dma = pltpu.SemaphoreType.DMA
+    smem = pltpu.SMEM
     scratch = [
+        smem(near_source.shape[::-1], jnp.int32),
+        smem(local_source.shape[::-1], jnp.int32),
+        smem(local_count.shape, jnp.int32),
+        smem(remote_source.shape, jnp.int32),
+        smem(top_source.shape[::-1], jnp.int32),
+        vmem(remote_target.shape, jnp.int32),
         vmem((boxes + 2 * HALO_LEAVES, points, vectors), BF16),
         vmem(leaf_basis.shape, BF16),
         vmem(leaf_transfer.shape, BF16),
@@ -550,7 +581,7 @@
         vmem((8, broad), jnp.int32),
         pltpu.SMEM((8, wide), jnp.int32),
         pltpu.SMEM((8, broad), jnp.int32),
-        dma((8,)),
+        dma((14,)),
         dma((4,)),
         dma((2,)),
         dma((2,)),
@@ -568,23 +599,22 @@
         dma((2, branch_size)),
         dma((2, branch_size)),
     ]
-    smem = pl.BlockSpec(memory_space=pltpu.SMEM)
     anywhere = pl.BlockSpec(memory_space=pl.ANY)
     return pl.pallas_call(
         functools.partial(kernel, branch_size, sub_size),
         out_shape=jax.ShapeDtypeStruct((boxes, points, vectors), BF16),
-        in_specs=[smem] * 5 + [pl.BlockSpec(memory_space=pltpu.VMEM)] + [anywhere] * 8,
+        in_specs=[anywhere] * 14,
         out_specs=anywhere,
         scratch_shapes=scratch,
         compiler_params=pltpu.CompilerParams(
             collective_id=0, has_side_effects=True, vmem_limit_bytes=60 * 2**20
         ),
     )(
-        near_source,
-        local_source,
+        near_source.T,
+        local_source.T,
         local_count,
         remote_source,
-        top_source,
+        top_source.T,
         remote_target,
         charges,
         leaf_basis,

time: 52.3 us -> 39.9 us (0.76); the launches traced: 51.4 us -> 39.8 us
  Pallas kernels: 45 us -> 37.5 us
  local copies, waits for them, and re-layouts: 6.36 us -> 2.26 us
    pallas_call x1, Pallas kernels: 45 us -> 37.5 us  [on_device(): pl.pallas_call(functools.partial(kernel, branch_size, sub_size), out_shap...]
    unnamed x4 -> x1, local copies, waits for them, and re-layouts: 6.36 us -> 2.26 us
where the time goes in v2:
time: 39.9 us; the launch traced here: 39.8 us
  Pallas kernels  37.5 us (94%)
  local copies, waits for them, and re-layouts  2.26 us (6%)
    pallas_call x1, Pallas kernels, on_device(): pl.pallas_call(functools.partial(kernel, branch_size, sub_size), out_shap...  37.5 us
    unnamed x1, local copies, waits for them, and re-layouts  2.26 us

profile of v2, /device:TPU:0, one launch (start us, length us, event | category | flops | bytes accessed | tf_op | source)
XLA Modules:
  0.0 39.8 jit_solution(1509574244599202787)
XLA Ops:
  0.0 37.5 %shard_map.136 = bf16[64,64,128]{2,1,0:T(8,128)(2,1)} custom-call(s32[8,64]{1,0:T(8,128)} %bitcast.3, s32[4,64]{1,0:T(4,128)} %bitcast.5, s32[64]{0:T(128)} %local_cnt_hbm.1, s32[1,32]{1,0:T(1,128)} %remote_src_hbm.1, s32[8,16]{1,0:T(8,128)} %bitcast.4, s32[1,32]{1,0:T(1,128)} %remote_tgt_hbm.1, bf16[64,64,128]{2,1,0:T(8,128)(2,1)} %charges_hbm.1, ...), custom_call_target="tpu_custom_call" | custom-call | tf_op jit(solution)/shard_map/pallas_call | solution.py:603
  37.5 2.3 %copy.16 = bf16[64,64,128]{2,1,0:T(8,128)(2,1)} copy(bf16[64,64,128]{2,1,0:T(8,128)(2,1)} %shard_map.136) | data formatting | bytes 2097152

commit v3 on v2

--- a/solution.py
+++ b/solution.py
@@ -85,7 +85,6 @@
     partials,
     tops,
     field,
-    leaf_field,
     result,
     label_tile,
     labels,
@@ -418,22 +417,6 @@
     prev_copy.start()
     last_copy.start()
 
-    def take_slots(i, carry):
-        slot_copy(me, peer_of(i)).wait_recv()
-        return carry
-
-    lax.fori_loop(1, devices, take_slots, 0)
-    prev_copy.wait()
-    last_copy.wait()
-    chain[slots] = jnp.zeros((rank, vectors), F32)
-
-    def link(s, carry):
-        value = arrived[lax.div(s, CAPACITY), lax.rem(s, CAPACITY)].astype(F32)
-        chain[s] = value + chain[prev_idx[0, s]]
-        return carry
-
-    lax.fori_loop(0, slots, link, 0)
-
     loads[7].wait()
     loads[13].wait()
     lax.fori_loop(0, branch_size, take_twin, 0)
@@ -468,13 +451,29 @@
     def put_leaf(p, value):
         for c in range(4):
             b = p * 4 + c
-            whole = value[c * rank : (c + 1) * rank] + local_field[b] + chain[last_idx[0, b]]
-            leaf_field[b] = whole.astype(BF16)
+            local_field[b] += value[c * rank : (c + 1) * rank]
 
     loop(0, parents, 2, lower, put_leaf)
 
+    def take_slots(i, carry):
+        slot_copy(me, peer_of(i)).wait_recv()
+        return carry
+
+    lax.fori_loop(1, devices, take_slots, 0)
+    prev_copy.wait()
+    last_copy.wait()
+    chain[slots] = jnp.zeros((rank, vectors), F32)
+
+    def link(s, carry):
+        value = arrived[lax.div(s, CAPACITY), lax.rem(s, CAPACITY)].astype(F32)
+        chain[s] = value + chain[prev_idx[0, s]]
+        return carry
+
+    lax.fori_loop(0, slots, link, 0)
+
     def potential(b):
-        return near_field[b] + jnp.dot(basis[b], leaf_field[b], preferred_element_type=F32)
+        leaf_field = (local_field[b] + chain[last_idx[0, b]]).astype(BF16)
+        return near_field[b] + jnp.dot(basis[b], leaf_field, preferred_element_type=F32)
 
     def put_result(b, value):
         result[b] = value.astype(BF16)
@@ -573,7 +572,6 @@
         vmem((sub_size, owned, rank, vectors), BF16),
         vmem((branch_size, sub_size, owned, rank, vectors), BF16),
         vmem((parents, rank, vectors), BF16),
-        vmem((boxes, rank, vectors), BF16),
         vmem((boxes, points, vectors), BF16),
         vmem((8, slots), jnp.int32),
         vmem((devices, 8, slots), jnp.int32),

time: 39.9 us -> 39.5 us (0.990)
  Pallas kernels: 37.5 us -> 37.1 us
    pallas_call x1, Pallas kernels: 37.5 us -> 37.1 us  [on_device(): pl.pallas_call(functools.partial(kernel, branch_size, sub_size), out_shap...]
where the time goes in v3:
time: 39.5 us; the launch traced here: 39.3 us
  Pallas kernels  37.1 us (94%)
  local copies, waits for them, and re-layouts  2.26 us (6%)
    pallas_call x1, Pallas kernels, on_device(): pl.pallas_call(functools.partial(kernel, branch_size, sub_size), out_shap...  37.1 us
    unnamed x1, local copies, waits for them, and re-layouts  2.26 us

profile of v3, /device:TPU:0, one launch (start us, length us, event | category | flops | bytes accessed | tf_op | source)
XLA Modules:
  0.0 39.3 jit_solution(17620609064725009460)
XLA Ops:
  0.0 37.1 %shard_map.136 = bf16[64,64,128]{2,1,0:T(8,128)(2,1)} custom-call(s32[8,64]{1,0:T(8,128)} %bitcast.3, s32[4,64]{1,0:T(4,128)} %bitcast.5, s32[64]{0:T(128)} %local_cnt_hbm.1, s32[1,32]{1,0:T(1,128)} %remote_src_hbm.1, s32[8,16]{1,0:T(8,128)} %bitcast.4, s32[1,32]{1,0:T(1,128)} %remote_tgt_hbm.1, bf16[64,64,128]{2,1,0:T(8,128)(2,1)} %charges_hbm.1, ...), custom_call_target="tpu_custom_call" | custom-call | tf_op jit(solution)/shard_map/pallas_call | solution.py:601
  37.1 2.3 %copy.16 = bf16[64,64,128]{2,1,0:T(8,128)(2,1)} copy(bf16[64,64,128]{2,1,0:T(8,128)(2,1)} %shard_map.136) | data formatting | bytes 2097152
